TPU v7x, 128 devices: a whole 4x4x4 slice. The times are simulated.
128 devices in a mesh: gx: 16 (over z, y_hi, core), gy: 8 (over x, y_lo).
Axes of the slice: x: 4, y: 4 (y_hi: 2, y_lo: 2; y = y_hi * 2 + y_lo), z: 4, core: 2. Of those that a mesh axis runs over, the one named last changes fastest.
Arguments:
- state: float32 [4, 256, 128, 128], P(None, 'gx', 'gy'), may hold values from -4 to 4
- offsets: int32 [2], replicated, may hold values from 0 to 127
Outputs:
- advanced: float32 [4, 256, 128, 128], P(None, 'gx', 'gy')
All inputs are finite; a program needn't handle non-finite values.
Results may differ from a plain program's by a relative error of at most 0.00002.
Values sent between devices are 32-bit elements; how exact they have to be, the bound alone decides.
A program may use at most 64 MiB of HBM per device.

v0:
```python
import jax
import jax.numpy as jnp
from jax import lax
from jax.sharding import PartitionSpec as P

RELAX = 4


time_step = 0.2
viscosity = 0.1


def from_behind(value, axis, steps):
    count = lax.axis_size(axis)
    pairs = [(source, (source + steps) % count) for source in range(count)]
    return lax.ppermute(value, axis, pairs)


def extended(x, sides, width):
    for axis, dim in sides:
        size, length = (lax.axis_size(axis), x.shape[dim])
        up = [(i, (i + 1) % size) for i in range(size)]
        down = [(j, i) for i, j in up]
        last = lax.slice_in_dim(x, length - width, length, axis=dim)
        first = lax.slice_in_dim(x, 0, width, axis=dim)
        before = lax.ppermute(last, axis, up)
        after = lax.ppermute(first, axis, down)
        x = jnp.concatenate([before, x, after], axis=dim)
    return x


def shrink(ext):
    return ext[..., 1:-1, 1:-1, :]


def diff_x(ext):
    return (ext[..., 2:, 1:-1, :] - ext[..., :-2, 1:-1, :]) * 0.5


def diff_y(ext):
    return (ext[..., 1:-1, 2:, :] - ext[..., 1:-1, :-2, :]) * 0.5


def diff_z(center):
    return (jnp.roll(center, -1, -1) - jnp.roll(center, 1, -1)) * 0.5


def beside_all(ext):
    center = shrink(ext)
    total = ext[..., 2:, 1:-1, :] + ext[..., :-2, 1:-1, :]
    total = total + ext[..., 1:-1, 2:, :] + ext[..., 1:-1, :-2, :]
    return total + jnp.roll(center, -1, -1) + jnp.roll(center, 1, -1)


def move_rows(planes, amount):
    rows = planes.shape[2]
    span = rows * lax.axis_size("gy")
    whole = lax.all_gather(planes, "gy", axis=2, tiled=True)
    doubled = jnp.concatenate([whole, whole], axis=2)
    start = (lax.axis_index("gy") * rows + amount) % span
    return lax.dynamic_slice_in_dim(doubled, start, rows, 2)


def ghost(field, offset, width):
    lower = from_behind(field[:, -width:], "gx", 1)
    upper = from_behind(field[:, :width], "gx", -1)
    place = lax.axis_index("gx")
    count = lax.axis_size("gx")
    span = field.shape[2] * lax.axis_size("gy")
    amount = jnp.where(place == 0, -offset, offset) % span
    moved = move_rows(jnp.concatenate([lower, upper], axis=1), amount)
    left = jnp.where(place == 0, moved[:, :width], lower)
    right = jnp.where(place == count - 1, moved[:, width:], upper)
    grown = jnp.concatenate([left, field, right], axis=1)
    return extended(grown, (("gy", 2),), width)


def advance(state, offset, xpos, shear, half_width):
    mean_flow = (shear * (xpos + 0.5 - half_width))[:, None, None]
    ext = ghost(state, offset, 1)
    speed_x, speed_y, speed_z = (state[0], state[1], state[2])
    carried = speed_x * diff_x(ext) + (speed_y + mean_flow) * diff_y(ext) + speed_z * diff_z(state)
    tendency = viscosity * (beside_all(ext) - 6.0 * state) - carried
    zeros = jnp.zeros_like(speed_x)
    source = jnp.stack([zeros, -shear * speed_x, zeros, -speed_x])
    provisional = state + time_step * (tendency + source)
    velo = ghost(provisional[:3], offset, 1)
    rhs = (diff_x(velo[0]) + diff_y(velo[1]) + diff_z(provisional[2])) / time_step
    pressure = -rhs / 6.0
    for sweep in range(RELAX):
        padded = ghost(pressure[None], offset, 1)[0]
        pressure = (beside_all(padded) - rhs) / 6.0
    padded = ghost(pressure[None], offset, 1)[0]
    new_x = provisional[0] - time_step * diff_x(padded)
    new_y = provisional[1] - time_step * diff_y(padded)
    new_z = provisional[2] - time_step * diff_z(pressure)
    return jnp.stack([new_x, new_y, new_z, provisional[3]])


def local(state, offsets):
    slab = state.shape[1]
    total_x = slab * lax.axis_size("gx")
    shear = 2.0 / total_x
    half_width = total_x / 2.0
    xpos = (lax.axis_index("gx") * slab + jnp.arange(slab)).astype(jnp.float32)
    for step in range(offsets.shape[0]):
        state = advance(state, offsets[step], xpos, shear, half_width)
    return state


def solution(mesh):
    in_specs = (P(None, "gx", "gy", None), P())
    out_specs = P(None, "gx", "gy", None)
    return jax.shard_map(local, mesh=mesh, in_specs=in_specs, out_specs=out_specs, check_vma=False)
```

profile of v0, /device:TPU:0, one launch (start us, length us, event | category | flops | bytes accessed | tf_op | source)
XLA Modules:
  0.0 597.1 jit_solution(2945560103122616609)
XLA Ops:
  0.8 6.3 %collective-permute-start.1 = (f32[4,1,16,128]{3,2,1,0:T(8,128)S(1)}, f32[4,1,16,128]{3,2,1,0:T(8,128)S(1)}, u32[]{:S(2)}, u32[]{:S(2)}) collective-permute-start(f32[4,1,16,128]{3,2,1,0:T(8,128)S(1)} %get-tuple-element.40), channel_id=1, source_target_pairs={{0,120},{8,0},{16,8},{24,16},{32,24},{40,32},{48,40},{56,48},{64,5... | collective-permute-start | bytes 98312 | tf_op jit(solution)/shard_map/ppermute | solution.py:16
  11.5 29.4 %all_gather.42 = f32[4,2,128,128]{3,0,1,2:T(4,128)S(1)} all-gather(f32[4,2,16,128]{3,0,1,2:T(4,128)S(1)} %copy.551), channel_id=1, replica_groups=mesh['gx'=16,'gy'=8] {'gy'}, dimensions={2}, use_global_device_ids=true | all-gather | bytes 589824 | tf_op jit(solution)/shard_map/all_gather | solution.py:58
  45.5 4.5 collective-permute-done.3
  50.8 5.3 collective-permute-start.5
  57.7 28.6 %all_gather.43 = f32[3,2,128,128]{3,1,0,2:T(2,128)S(1)} all-gather(f32[3,2,16,128]{3,1,0,2:T(2,128)S(1)} %copy.558), channel_id=1, replica_groups=mesh['gx'=16,'gy'=8] {'gy'}, dimensions={2}, use_global_device_ids=true | all-gather | bytes 442368 | tf_op jit(solution)/shard_map/all_gather | solution.py:58
  86.5 4.1 collective-permute-start.7
  92.8 5.3 collective-permute-start.9
  99.5 28.2 %all_gather.44 = f32[1,2,128,128]{3,1,0,2:T(2,128)S(1)} all-gather(f32[1,2,16,128]{3,1,0,2:T(2,128)S(1)} %copy.561), channel_id=1, replica_groups=mesh['gx'=16,'gy'=8] {'gy'}, dimensions={2}, use_global_device_ids=true | all-gather | bytes 147456 | tf_op jit(solution)/shard_map/all_gather | solution.py:58
  134.2 5.3 collective-permute-start.13
  140.9 28.3 %all_gather.45 = f32[1,2,128,128]{3,1,0,2:T(2,128)S(1)} all-gather(f32[1,2,16,128]{3,1,0,2:T(2,128)S(1)} %copy.564), channel_id=1, replica_groups=mesh['gx'=16,'gy'=8] {'gy'}, dimensions={2}, use_global_device_ids=true | all-gather | bytes 147456 | tf_op jit(solution)/shard_map/all_gather | solution.py:58
  175.6 5.3 collective-permute-start.17
  182.4 28.2 %all_gather.46 = f32[1,2,128,128]{3,1,0,2:T(2,128)S(1)} all-gather(f32[1,2,16,128]{3,1,0,2:T(2,128)S(1)} %copy.567), channel_id=1, replica_groups=mesh['gx'=16,'gy'=8] {'gy'}, dimensions={2}, use_global_device_ids=true | all-gather | bytes 147456 | tf_op jit(solution)/shard_map/all_gather | solution.py:58
  217.1 5.3 collective-permute-start.21
  223.9 28.2 %all_gather.47 = f32[1,2,128,128]{3,1,0,2:T(2,128)S(1)} all-gather(f32[1,2,16,128]{3,1,0,2:T(2,128)S(1)} %copy.570), channel_id=1, replica_groups=mesh['gx'=16,'gy'=8] {'gy'}, dimensions={2}, use_global_device_ids=true | all-gather | bytes 147456 | tf_op jit(solution)/shard_map/all_gather | solution.py:58
  258.6 5.3 collective-permute-start.25
  265.4 28.2 %all_gather.48 = f32[1,2,128,128]{3,1,0,2:T(2,128)S(1)} all-gather(f32[1,2,16,128]{3,1,0,2:T(2,128)S(1)} %copy.573), channel_id=1, replica_groups=mesh['gx'=16,'gy'=8] {'gy'}, dimensions={2}, use_global_device_ids=true | all-gather | bytes 147456 | tf_op jit(solution)/shard_map/all_gather | solution.py:58
  300.0 5.3 collective-permute-start.29
  307.2 28.9 %all_gather.49 = f32[4,2,128,128]{3,0,1,2:T(4,128)S(1)} all-gather(f32[4,2,16,128]{3,0,1,2:T(4,128)S(1)} %copy.578), channel_id=1, replica_groups=mesh['gx'=16,'gy'=8] {'gy'}, dimensions={2}, use_global_device_ids=true | all-gather | bytes 589824 | tf_op jit(solution)/shard_map/all_gather | solution.py:58
  336.4 4.2 collective-permute-start.30
  342.3 4.5 collective-permute-done.31
  347.5 5.3 collective-permute-start.33
  354.4 28.7 %all_gather.50 = f32[3,2,128,128]{3,1,0,2:T(2,128)S(1)} all-gather(f32[3,2,16,128]{3,1,0,2:T(2,128)S(1)} %copy.585), channel_id=1, replica_groups=mesh['gx'=16,'gy'=8] {'gy'}, dimensions={2}, use_global_device_ids=true | all-gather | bytes 442368 | tf_op jit(solution)/shard_map/all_gather | solution.py:58
  389.6 5.3 collective-permute-start.37
  396.3 28.2 %all_gather.51 = f32[1,2,128,128]{3,1,0,2:T(2,128)S(1)} all-gather(f32[1,2,16,128]{3,1,0,2:T(2,128)S(1)} %copy.588), channel_id=1, replica_groups=mesh['gx'=16,'gy'=8] {'gy'}, dimensions={2}, use_global_device_ids=true | all-gather | bytes 147456 | tf_op jit(solution)/shard_map/all_gather | solution.py:58
  430.9 5.3 collective-permute-start.41
  437.7 28.2 %all_gather.52 = f32[1,2,128,128]{3,1,0,2:T(2,128)S(1)} all-gather(f32[1,2,16,128]{3,1,0,2:T(2,128)S(1)} %copy.591), channel_id=1, replica_groups=mesh['gx'=16,'gy'=8] {'gy'}, dimensions={2}, use_global_device_ids=true | all-gather | bytes 147456 | tf_op jit(solution)/shard_map/all_gather | solution.py:58
  472.3 5.3 collective-permute-start.45
  479.1 28.2 %all_gather.53 = f32[1,2,128,128]{3,1,0,2:T(2,128)S(1)} all-gather(f32[1,2,16,128]{3,1,0,2:T(2,128)S(1)} %copy.594), channel_id=1, replica_groups=mesh['gx'=16,'gy'=8] {'gy'}, dimensions={2}, use_global_device_ids=true | all-gather | bytes 147456 | tf_op jit(solution)/shard_map/all_gather | solution.py:58
  513.7 5.3 collective-permute-start.49
  520.5 28.2 %all_gather.54 = f32[1,2,128,128]{3,1,0,2:T(2,128)S(1)} all-gather(f32[1,2,16,128]{3,1,0,2:T(2,128)S(1)} %copy.597), channel_id=1, replica_groups=mesh['gx'=16,'gy'=8] {'gy'}, dimensions={2}, use_global_device_ids=true | all-gather | bytes 147456 | tf_op jit(solution)/shard_map/all_gather | solution.py:58
  555.2 5.3 collective-permute-start.53
  562.0 28.2 %all_gather.55 = f32[1,2,128,128]{3,1,0,2:T(2,128)S(1)} all-gather(f32[1,2,16,128]{3,1,0,2:T(2,128)S(1)} %copy.600), channel_id=1, replica_groups=mesh['gx'=16,'gy'=8] {'gy'}, dimensions={2}, use_global_device_ids=true | all-gather | bytes 147456 | tf_op jit(solution)/shard_map/all_gather | solution.py:58
  (271 shorter events, 102.3 us)
Async XLA Ops:
  0.8 10.7 %collective-permute-start = (f32[4,1,16,128]{3,2,1,0:T(8,128)S(1)}, f32[4,1,16,128]{3,2,1,0:T(8,128)S(1)}, u32[]{:S(2)}, u32[]{:S(2)}) collective-permute-start(f32[4,1,16,128]{3,2,1,0:T(8,128)S(1)} %get-tuple-element.39), channel_id=1, source_target_pairs={{0,8},{8,16},{16,24},{24,32},{32,40},{40,48},{48,56},{56,64},{64,7... | collective-permute-start | bytes 98312 | tf_op jit(solution)/shard_map/ppermute | solution.py:16
  0.8 10.7 %collective-permute-start.1 = (f32[4,1,16,128]{3,2,1,0:T(8,128)S(1)}, f32[4,1,16,128]{3,2,1,0:T(8,128)S(1)}, u32[]{:S(2)}, u32[]{:S(2)}) collective-permute-start(f32[4,1,16,128]{3,2,1,0:T(8,128)S(1)} %get-tuple-element.40), channel_id=1, source_target_pairs={{0,120},{8,0},{16,8},{24,16},{32,24},{40,32},{48,40},{56,48},{64,5... | collective-permute-start | bytes 98312 | tf_op jit(solution)/shard_map/ppermute | solution.py:16
  43.8 6.1 %collective-permute-start.3 = (f32[4,18,1,128]{3,0,2,1:T(4,128)S(1)}, f32[4,18,1,128]{3,0,2,1:T(4,128)S(1)}, u32[]{:S(2)}, u32[]{:S(2)}) collective-permute-start(f32[4,18,1,128]{3,0,2,1:T(4,128)S(1)} %copy.556), channel_id=1, source_target_pairs={{0,1},{1,2},{2,3},{3,4},{4,5},{5,6},{6,7},{7,0},{8,9},{9,10},{10,1... | collective-permute-start | bytes 110600 | tf_op jit(solution)/shard_map/ppermute | solution.py:26
  50.7 6.9 %collective-permute-start.4 = (f32[3,1,16,128]{3,2,1,0:T(8,128)S(1)}, f32[3,1,16,128]{3,2,1,0:T(8,128)S(1)}, u32[]{:S(2)}, u32[]{:S(2)}) collective-permute-start(f32[3,1,16,128]{3,2,1,0:T(8,128)S(1)} %get-tuple-element.32), channel_id=1, source_target_pairs={{0,8},{8,16},{16,24},{24,32},{32,40},{40,48},{48,56},{56,64},{64,7... | collective-permute-start | bytes 73736 | tf_op jit(solution)/shard_map/ppermute | solution.py:16
  50.8 6.9 %collective-permute-start.5 = (f32[3,1,16,128]{3,2,1,0:T(8,128)S(1)}, f32[3,1,16,128]{3,2,1,0:T(8,128)S(1)}, u32[]{:S(2)}, u32[]{:S(2)}) collective-permute-start(f32[3,1,16,128]{3,2,1,0:T(8,128)S(1)} %get-tuple-element.33), channel_id=1, source_target_pairs={{0,120},{8,0},{16,8},{24,16},{32,24},{40,32},{48,40},{56,48},{64,5... | collective-permute-start | bytes 73736 | tf_op jit(solution)/shard_map/ppermute | solution.py:16
  86.5 6.0 %collective-permute-start.6 = (f32[3,18,1,128]{3,2,1,0:T(1,128)S(1)}, f32[3,18,1,128]{3,2,1,0:T(1,128)S(1)}, u32[]{:S(2)}, u32[]{:S(2)}) collective-permute-start(f32[3,18,1,128]{3,2,1,0:T(1,128)S(1)} %get-tuple-element.51), channel_id=1, source_target_pairs={{0,1},{1,2},{2,3},{3,4},{4,5},{5,6},{6,7},{7,0},{8,9},{9,10},{10,1... | collective-permute-start | bytes 82952 | tf_op jit(solution)/shard_map/ppermute | solution.py:26
  92.7 6.8 %collective-permute-start.8 = (f32[1,1,16,128]{3,2,1,0:T(8,128)S(1)}, f32[1,1,16,128]{3,2,1,0:T(8,128)S(1)}, u32[]{:S(2)}, u32[]{:S(2)}) collective-permute-start(f32[1,1,16,128]{3,2,1,0:T(8,128)S(1)} %get-tuple-element.137), channel_id=1, source_target_pairs={{0,8},{8,16},{16,24},{24,32},{32,40},{40,48},{48,56},{56,64},{64,7... | collective-permute-start | bytes 24584 | tf_op jit(solution)/shard_map/ppermute | solution.py:16
  92.8 6.7 %collective-permute-start.9 = (f32[1,1,16,128]{3,2,1,0:T(8,128)S(1)}, f32[1,1,16,128]{3,2,1,0:T(8,128)S(1)}, u32[]{:S(2)}, u32[]{:S(2)}) collective-permute-start(f32[1,1,16,128]{3,2,1,0:T(8,128)S(1)} %get-tuple-element.138), channel_id=1, source_target_pairs={{0,120},{8,0},{16,8},{24,16},{32,24},{40,32},{48,40},{56,48},{64,5... | collective-permute-start | bytes 24584 | tf_op jit(solution)/shard_map/ppermute | solution.py:16
  134.1 6.8 %collective-permute-start.12 = (f32[1,1,16,128]{3,2,1,0:T(8,128)S(1)}, f32[1,1,16,128]{3,2,1,0:T(8,128)S(1)}, u32[]{:S(2)}, u32[]{:S(2)}) collective-permute-start(f32[1,1,16,128]{3,2,1,0:T(8,128)S(1)} %get-tuple-element.135), channel_id=1, source_target_pairs={{0,8},{8,16},{16,24},{24,32},{32,40},{40,48},{48,56},{56,64},{64,7... | collective-permute-start | bytes 24584 | tf_op jit(solution)/shard_map/ppermute | solution.py:16
  134.2 6.7 %collective-permute-start.13 = (f32[1,1,16,128]{3,2,1,0:T(8,128)S(1)}, f32[1,1,16,128]{3,2,1,0:T(8,128)S(1)}, u32[]{:S(2)}, u32[]{:S(2)}) collective-permute-start(f32[1,1,16,128]{3,2,1,0:T(8,128)S(1)} %get-tuple-element.136), channel_id=1, source_target_pairs={{0,120},{8,0},{16,8},{24,16},{32,24},{40,32},{48,40},{56,48},{64,5... | collective-permute-start | bytes 24584 | tf_op jit(solution)/shard_map/ppermute | solution.py:16
  175.5 6.8 %collective-permute-start.16 = (f32[1,1,16,128]{3,2,1,0:T(8,128)S(1)}, f32[1,1,16,128]{3,2,1,0:T(8,128)S(1)}, u32[]{:S(2)}, u32[]{:S(2)}) collective-permute-start(f32[1,1,16,128]{3,2,1,0:T(8,128)S(1)} %get-tuple-element.133), channel_id=1, source_target_pairs={{0,8},{8,16},{16,24},{24,32},{32,40},{40,48},{48,56},{56,64},{64,7... | collective-permute-start | bytes 24584 | tf_op jit(solution)/shard_map/ppermute | solution.py:16
  175.6 6.7 %collective-permute-start.17 = (f32[1,1,16,128]{3,2,1,0:T(8,128)S(1)}, f32[1,1,16,128]{3,2,1,0:T(8,128)S(1)}, u32[]{:S(2)}, u32[]{:S(2)}) collective-permute-start(f32[1,1,16,128]{3,2,1,0:T(8,128)S(1)} %get-tuple-element.134), channel_id=1, source_target_pairs={{0,120},{8,0},{16,8},{24,16},{32,24},{40,32},{48,40},{56,48},{64,5... | collective-permute-start | bytes 24584 | tf_op jit(solution)/shard_map/ppermute | solution.py:16
  216.9 6.9 %collective-permute-start.20 = (f32[1,1,16,128]{3,2,1,0:T(8,128)S(1)}, f32[1,1,16,128]{3,2,1,0:T(8,128)S(1)}, u32[]{:S(2)}, u32[]{:S(2)}) collective-permute-start(f32[1,1,16,128]{3,2,1,0:T(8,128)S(1)} %get-tuple-element.131), channel_id=1, source_target_pairs={{0,8},{8,16},{16,24},{24,32},{32,40},{40,48},{48,56},{56,64},{64,7... | collective-permute-start | bytes 24584 | tf_op jit(solution)/shard_map/ppermute | solution.py:16
  217.1 6.7 %collective-permute-start.21 = (f32[1,1,16,128]{3,2,1,0:T(8,128)S(1)}, f32[1,1,16,128]{3,2,1,0:T(8,128)S(1)}, u32[]{:S(2)}, u32[]{:S(2)}) collective-permute-start(f32[1,1,16,128]{3,2,1,0:T(8,128)S(1)} %get-tuple-element.132), channel_id=1, source_target_pairs={{0,120},{8,0},{16,8},{24,16},{32,24},{40,32},{48,40},{56,48},{64,5... | collective-permute-start | bytes 24584 | tf_op jit(solution)/shard_map/ppermute | solution.py:16
  258.6 6.8 %collective-permute-start.24 = (f32[1,1,16,128]{3,2,1,0:T(8,128)S(1)}, f32[1,1,16,128]{3,2,1,0:T(8,128)S(1)}, u32[]{:S(2)}, u32[]{:S(2)}) collective-permute-start(f32[1,1,16,128]{3,2,1,0:T(8,128)S(1)} %get-tuple-element.129), channel_id=1, source_target_pairs={{0,8},{8,16},{16,24},{24,32},{32,40},{40,48},{48,56},{56,64},{64,7... | collective-permute-start | bytes 24584 | tf_op jit(solution)/shard_map/ppermute | solution.py:16
  258.6 6.7 %collective-permute-start.25 = (f32[1,1,16,128]{3,2,1,0:T(8,128)S(1)}, f32[1,1,16,128]{3,2,1,0:T(8,128)S(1)}, u32[]{:S(2)}, u32[]{:S(2)}) collective-permute-start(f32[1,1,16,128]{3,2,1,0:T(8,128)S(1)} %get-tuple-element.130), channel_id=1, source_target_pairs={{0,120},{8,0},{16,8},{24,16},{32,24},{40,32},{48,40},{56,48},{64,5... | collective-permute-start | bytes 24584 | tf_op jit(solution)/shard_map/ppermute | solution.py:16
  299.9 7.0 %collective-permute-start.28 = (f32[4,1,16,128]{3,2,1,0:T(8,128)S(1)}, f32[4,1,16,128]{3,2,1,0:T(8,128)S(1)}, u32[]{:S(2)}, u32[]{:S(2)}) collective-permute-start(f32[4,1,16,128]{3,2,1,0:T(8,128)S(1)} %get-tuple-element.25), channel_id=1, source_target_pairs={{0,8},{8,16},{16,24},{24,32},{32,40},{40,48},{48,56},{56,64},{64,7... | collective-permute-start | bytes 98312 | tf_op jit(solution)/shard_map/ppermute | solution.py:16
  300.0 7.1 %collective-permute-start.29 = (f32[4,1,16,128]{3,2,1,0:T(8,128)S(1)}, f32[4,1,16,128]{3,2,1,0:T(8,128)S(1)}, u32[]{:S(2)}, u32[]{:S(2)}) collective-permute-start(f32[4,1,16,128]{3,2,1,0:T(8,128)S(1)} %get-tuple-element.26), channel_id=1, source_target_pairs={{0,120},{8,0},{16,8},{24,16},{32,24},{40,32},{48,40},{56,48},{64,5... | collective-permute-start | bytes 98312 | tf_op jit(solution)/shard_map/ppermute | solution.py:16
  340.6 6.1 %collective-permute-start.31 = (f32[4,18,1,128]{3,0,2,1:T(4,128)S(1)}, f32[4,18,1,128]{3,0,2,1:T(4,128)S(1)}, u32[]{:S(2)}, u32[]{:S(2)}) collective-permute-start(f32[4,18,1,128]{3,0,2,1:T(4,128)S(1)} %copy.583), channel_id=1, source_target_pairs={{0,1},{1,2},{2,3},{3,4},{4,5},{5,6},{6,7},{7,0},{8,9},{9,10},{10,1... | collective-permute-start | bytes 110600 | tf_op jit(solution)/shard_map/ppermute | solution.py:26
  347.4 6.9 %collective-permute-start.32 = (f32[3,1,16,128]{3,2,1,0:T(8,128)S(1)}, f32[3,1,16,128]{3,2,1,0:T(8,128)S(1)}, u32[]{:S(2)}, u32[]{:S(2)}) collective-permute-start(f32[3,1,16,128]{3,2,1,0:T(8,128)S(1)} %get-tuple-element.23), channel_id=1, source_target_pairs={{0,8},{8,16},{16,24},{24,32},{32,40},{40,48},{48,56},{56,64},{64,7... | collective-permute-start | bytes 73736 | tf_op jit(solution)/shard_map/ppermute | solution.py:16
  347.5 6.9 %collective-permute-start.33 = (f32[3,1,16,128]{3,2,1,0:T(8,128)S(1)}, f32[3,1,16,128]{3,2,1,0:T(8,128)S(1)}, u32[]{:S(2)}, u32[]{:S(2)}) collective-permute-start(f32[3,1,16,128]{3,2,1,0:T(8,128)S(1)} %get-tuple-element.24), channel_id=1, source_target_pairs={{0,120},{8,0},{16,8},{24,16},{32,24},{40,32},{48,40},{56,48},{64,5... | collective-permute-start | bytes 73736 | tf_op jit(solution)/shard_map/ppermute | solution.py:16
  383.2 6.0 %collective-permute-start.34 = (f32[3,18,1,128]{3,2,1,0:T(1,128)S(1)}, f32[3,18,1,128]{3,2,1,0:T(1,128)S(1)}, u32[]{:S(2)}, u32[]{:S(2)}) collective-permute-start(f32[3,18,1,128]{3,2,1,0:T(1,128)S(1)} %get-tuple-element.49), channel_id=1, source_target_pairs={{0,1},{1,2},{2,3},{3,4},{4,5},{5,6},{6,7},{7,0},{8,9},{9,10},{10,1... | collective-permute-start | bytes 82952 | tf_op jit(solution)/shard_map/ppermute | solution.py:26
  389.5 6.8 %collective-permute-start.36 = (f32[1,1,16,128]{3,2,1,0:T(8,128)S(1)}, f32[1,1,16,128]{3,2,1,0:T(8,128)S(1)}, u32[]{:S(2)}, u32[]{:S(2)}) collective-permute-start(f32[1,1,16,128]{3,2,1,0:T(8,128)S(1)} %get-tuple-element.117), channel_id=1, source_target_pairs={{0,8},{8,16},{16,24},{24,32},{32,40},{40,48},{48,56},{56,64},{64,7... | collective-permute-start | bytes 24584 | tf_op jit(solution)/shard_map/ppermute | solution.py:16
  389.6 6.7 %collective-permute-start.37 = (f32[1,1,16,128]{3,2,1,0:T(8,128)S(1)}, f32[1,1,16,128]{3,2,1,0:T(8,128)S(1)}, u32[]{:S(2)}, u32[]{:S(2)}) collective-permute-start(f32[1,1,16,128]{3,2,1,0:T(8,128)S(1)} %get-tuple-element.118), channel_id=1, source_target_pairs={{0,120},{8,0},{16,8},{24,16},{32,24},{40,32},{48,40},{56,48},{64,5... | collective-permute-start | bytes 24584 | tf_op jit(solution)/shard_map/ppermute | solution.py:16
  430.8 6.8 %collective-permute-start.40 = (f32[1,1,16,128]{3,2,1,0:T(8,128)S(1)}, f32[1,1,16,128]{3,2,1,0:T(8,128)S(1)}, u32[]{:S(2)}, u32[]{:S(2)}) collective-permute-start(f32[1,1,16,128]{3,2,1,0:T(8,128)S(1)} %get-tuple-element.115), channel_id=1, source_target_pairs={{0,8},{8,16},{16,24},{24,32},{32,40},{40,48},{48,56},{56,64},{64,7... | collective-permute-start | bytes 24584 | tf_op jit(solution)/shard_map/ppermute | solution.py:16
  430.9 6.7 %collective-permute-start.41 = (f32[1,1,16,128]{3,2,1,0:T(8,128)S(1)}, f32[1,1,16,128]{3,2,1,0:T(8,128)S(1)}, u32[]{:S(2)}, u32[]{:S(2)}) collective-permute-start(f32[1,1,16,128]{3,2,1,0:T(8,128)S(1)} %get-tuple-element.116), channel_id=1, source_target_pairs={{0,120},{8,0},{16,8},{24,16},{32,24},{40,32},{48,40},{56,48},{64,5... | collective-permute-start | bytes 24584 | tf_op jit(solution)/shard_map/ppermute | solution.py:16
  472.2 6.8 %collective-permute-start.44 = (f32[1,1,16,128]{3,2,1,0:T(8,128)S(1)}, f32[1,1,16,128]{3,2,1,0:T(8,128)S(1)}, u32[]{:S(2)}, u32[]{:S(2)}) collective-permute-start(f32[1,1,16,128]{3,2,1,0:T(8,128)S(1)} %get-tuple-element.113), channel_id=1, source_target_pairs={{0,8},{8,16},{16,24},{24,32},{32,40},{40,48},{48,56},{56,64},{64,7... | collective-permute-start | bytes 24584 | tf_op jit(solution)/shard_map/ppermute | solution.py:16
  472.3 6.7 %collective-permute-start.45 = (f32[1,1,16,128]{3,2,1,0:T(8,128)S(1)}, f32[1,1,16,128]{3,2,1,0:T(8,128)S(1)}, u32[]{:S(2)}, u32[]{:S(2)}) collective-permute-start(f32[1,1,16,128]{3,2,1,0:T(8,128)S(1)} %get-tuple-element.114), channel_id=1, source_target_pairs={{0,120},{8,0},{16,8},{24,16},{32,24},{40,32},{48,40},{56,48},{64,5... | collective-permute-start | bytes 24584 | tf_op jit(solution)/shard_map/ppermute | solution.py:16
  513.6 6.8 %collective-permute-start.48 = (f32[1,1,16,128]{3,2,1,0:T(8,128)S(1)}, f32[1,1,16,128]{3,2,1,0:T(8,128)S(1)}, u32[]{:S(2)}, u32[]{:S(2)}) collective-permute-start(f32[1,1,16,128]{3,2,1,0:T(8,128)S(1)} %get-tuple-element.111), channel_id=1, source_target_pairs={{0,8},{8,16},{16,24},{24,32},{32,40},{40,48},{48,56},{56,64},{64,7... | collective-permute-start | bytes 24584 | tf_op jit(solution)/shard_map/ppermute | solution.py:16
  513.7 6.7 %collective-permute-start.49 = (f32[1,1,16,128]{3,2,1,0:T(8,128)S(1)}, f32[1,1,16,128]{3,2,1,0:T(8,128)S(1)}, u32[]{:S(2)}, u32[]{:S(2)}) collective-permute-start(f32[1,1,16,128]{3,2,1,0:T(8,128)S(1)} %get-tuple-element.112), channel_id=1, source_target_pairs={{0,120},{8,0},{16,8},{24,16},{32,24},{40,32},{48,40},{56,48},{64,5... | collective-permute-start | bytes 24584 | tf_op jit(solution)/shard_map/ppermute | solution.py:16
  555.1 6.8 %collective-permute-start.52 = (f32[1,1,16,128]{3,2,1,0:T(8,128)S(1)}, f32[1,1,16,128]{3,2,1,0:T(8,128)S(1)}, u32[]{:S(2)}, u32[]{:S(2)}) collective-permute-start(f32[1,1,16,128]{3,2,1,0:T(8,128)S(1)} %get-tuple-element.105), channel_id=1, source_target_pairs={{0,8},{8,16},{16,24},{24,32},{32,40},{40,48},{48,56},{56,64},{64,7... | collective-permute-start | bytes 24584 | tf_op jit(solution)/shard_map/ppermute | solution.py:16
  555.2 6.7 %collective-permute-start.53 = (f32[1,1,16,128]{3,2,1,0:T(8,128)S(1)}, f32[1,1,16,128]{3,2,1,0:T(8,128)S(1)}, u32[]{:S(2)}, u32[]{:S(2)}) collective-permute-start(f32[1,1,16,128]{3,2,1,0:T(8,128)S(1)} %get-tuple-element.106), channel_id=1, source_target_pairs={{0,120},{8,0},{16,8},{24,16},{32,24},{40,32},{48,40},{56,48},{64,5... | collective-permute-start | bytes 24584 | tf_op jit(solution)/shard_map/ppermute | solution.py:16
  (26 other events, 120.5 us)
where the time goes:
time: 598 us; the launch traced here: 597 us
  blocking collectives  398 us (67%)
  starting transfers between devices  135 us (23%)
  waiting for transfers between devices  47.4 us (8%)
  local copies, waits for them, and re-layouts  7.43 us (1%)
    all_gather x14, blocking collectives, move_rows(): whole = lax.all_gather(planes, 'gy', axis=2, tiled=True)  398 us
    ppermute x28, starting transfers between devices, from_behind(): return lax.ppermute(value, axis, pairs)  76.9 us
    ppermute x14, starting transfers between devices, extended(): after = lax.ppermute(first, axis, down)  37 us
    ppermute x14, waiting for transfers between devices, extended(): before = lax.ppermute(last, axis, up)  26.6 us
    ppermute x14, starting transfers between devices, extended(): before = lax.ppermute(last, axis, up)  21 us
    ppermute x28, waiting for transfers between devices, from_behind(): return lax.ppermute(value, axis, pairs)  17.8 us
  transfers between devices with their start and end apart: 56, of which 30 were waited for; matrix products, arithmetic and copies ran while one was open for 1% of the time, Pallas kernels for 0%

commit v1 on v0

v1 whole, which is shorter than its diff:
```python
import functools

import jax
import jax.numpy as jnp
from jax import lax
from jax.experimental import pallas as pl
from jax.experimental.pallas import tpu as pltpu
from jax.sharding import PartitionSpec as P

RELAX = 4
DEEP = RELAX + 1

time_step = 0.2
viscosity = 0.1

MESH = pl.DeviceIdType.MESH
ROW = 8
TALL = 32


def across(x, shift):
    return pltpu.roll(x, shift % x.shape[-1], x.ndim - 1)


def stencil(c, xm, xp, ym, yp):
    zp, zm = across(c, -1), across(c, 1)
    total = (xp + xm) + (yp + ym) + (zp + zm)
    return total, xp - xm, yp - ym, zp - zm


def kernel(ngx, ngy, steps, offsets, state, out, ext, prov, rhs, press, final,
           x_send, x_recv, y_send, y_recv, c_send, c_recv, send_sem, recv_sem, shear_out, shear_in, local_sem, *shear_recv):
    slab, rows = state.shape[1], state.shape[2]
    gx, gy = lax.axis_index("gx"), lax.axis_index("gy")
    below, above = lax.rem(gx + ngx - 1, ngx), lax.rem(gx + 1, ngx)
    left, right = lax.rem(gy + ngy - 1, ngy), lax.rem(gy + 1, ngy)
    at_x = {-1: below, 0: gx, 1: above}
    at_y = {-1: left, 0: gy, 1: right}
    has = {-1: gx > 0, 1: gx < ngx - 1}
    ends = {-1: gx == 0, 1: gx == ngx - 1}
    far = {-1: ngx - 1, 1: 0}
    total_x = slab * ngx
    rate = 2.0 / total_x
    own = pl.ds(ROW, rows)

    fetch = pltpu.make_async_copy(state, ext.at[0, :, pl.ds(2, slab), own, :], local_sem.at[0])
    fetch.start()

    barrier = pltpu.get_barrier_semaphore()

    def greet(x, y):
        pl.semaphore_signal(barrier, inc=1, device_id=(x, y), device_id_type=MESH)

    for dy in (-1, 1):
        greet(gx, at_y[dy])
    for dx in (-1, 1):
        @pl.when(has[dx])
        def _():
            for dy in (-1, 0, 1):
                greet(at_x[dx], at_y[dy])

        @pl.when(ends[dx])
        def _():
            for k in range(ngy):
                greet(far[dx], k)

    def remote(src, dst, send, recv, x, y):
        return pltpu.make_async_remote_copy(
            src_ref=src, dst_ref=dst, send_sem=send, recv_sem=recv,
            device_id=(x, y), device_id_type=MESH)

    def rim(side, width, size):
        return (0, size) if side < 0 else (size - width, -width)

    def messages(step, part, dx, dy):
        dev = at_x[dx], at_y[dy]
        if dx == 0:
            n = m = (dy + 1) // 2
            src, dst = y_send.at[step, part, m], y_recv.at[step, part, m]
        elif dy == 0:
            m = (dx + 1) // 2
            n = 2 + m
            src, dst = x_send.at[step, part, m], x_recv.at[step, part, m]
        else:
            m = (dx + 1) + (dy + 1) // 2
            n = 4 + m
            size = pl.ds(0, 8 if part == 0 else 16)
            src, dst = c_send.at[step, part, m, size, :], c_recv.at[step, part, m, size, :]
        return remote(src, dst, send_sem.at[step, part, n], recv_sem.at[step, part, n], *dev)

    def shear_slot(step, part, k):
        return shear_recv[2 * step + part].at[:, pl.ds(k * (rows // 8), rows // 8), :, :]

    def shear_message(step, part, dx, k):
        return remote(x_send.at[step, part, (dx + 1) // 2], shear_slot(step, part, gy),
                      shear_out.at[step, part, k], shear_in.at[step, part, gy], far[dx], k)

    def shear_arrival(step, part, dx, k):
        slot = shear_slot(step, part, k)
        return remote(slot, slot, shear_out.at[step, part, k], shear_in.at[step, part, k], far[dx], k)

    def field_planes(dx, ghost):
        s2, d2 = rim(dx, 2, slab)
        s1, d1 = rim(dx, 1, slab)
        p2, p1 = (d2, d1) if ghost else (s2, s1)
        return [(0, 2 + p2), (0, 3 + p2), (1, 2 + p1), (2, 2 + p1), (3, 2 + p1)]

    def lines(part, dy, ghost):
        if part == 0:
            s2, d2 = rim(dy, 2, rows)
            s1, d1 = rim(dy, 1, rows)
            p2, p1 = (d2, d1) if ghost else (s2, s1)
            return [(f * (slab + 4) + 2) * TALL + ROW + y
                    for f, y in ((1, p2), (1, p2 + 1), (0, p1), (2, p1), (3, p1))]
        s, d = rim(dy, DEEP, rows)
        return [DEEP * TALL + ROW + (d if ghost else s) + k for k in range(DEEP)]

    def flattened(step, part):
        if part == 0:
            return ext.at[step].reshape(4 * (slab + 4) * TALL, 128)
        return rhs.at[step].reshape((slab + 2 * DEEP) * TALL, 128)

    def pack(step, part):
        for dx in (-1, 1):
            m = (dx + 1) // 2
            for n in range(DEEP):
                if part == 0:
                    f, X = field_planes(dx, False)[n]
                else:
                    X = DEEP + rim(dx, DEEP, slab)[0] + n
                for c in range(rows // 8):
                    piece = slice(ROW + 8 * c, ROW + 8 * c + 8)
                    x_send[step, part, m, n, c] = ext[step, f, X, piece] if part == 0 else rhs[step, X, piece]
        flat = flattened(step, part)
        for dy in (-1, 1):
            for n, base in enumerate(lines(part, dy, False)):
                y_send[step, part, (dy + 1) // 2, n] = flat[pl.ds(base, slab, stride=TALL), :]
        w = 1 if part == 0 else DEEP - 1
        for dx in (-1, 1):
            for dy in (-1, 1):
                m = (dx + 1) + (dy + 1) // 2
                x, y = rim(dx, w, slab)[0], ROW + rim(dy, w, rows)[0]
                if part == 0:
                    for f in range(2):
                        c_send[step, part, m, f:f + 1] = ext[step, f, 2 + x, y:y + 1]
                else:
                    for n in range(w):
                        c_send[step, part, m, w * n:w * n + w] = rhs[step, DEEP + x + n, y:y + w]

    def start_all(step, part):
        for dx in (-1, 1):
            @pl.when(ends[dx])
            def _():
                for k in range(ngy):
                    shear_message(step, part, dx, k).start()
        for dx in (-1, 1):
            @pl.when(has[dx])
            def _():
                for dy in (0, -1, 1):
                    messages(step, part, dx, dy).start()
        for dy in (-1, 1):
            messages(step, part, 0, dy).start()

    def sheared(step, part, dx):
        span = rows * ngy
        shift = span - offsets[step] if dx > 0 else offsets[step]
        start = lax.rem(gy * rows + shift + (span - ROW), span)
        block, within = lax.div(start, 8), lax.rem(start, 8)
        blocks = [lax.rem(block + c, span // 8) for c in range(TALL // 8 + 1)]
        for n in range(DEEP):
            tall = jnp.concatenate([shear_recv[2 * step + part][n, at] for at in blocks], axis=0)
            plane = pltpu.roll(tall, TALL + 8 - within, 0)[:TALL]
            if part == 0:
                f, X = field_planes(dx, True)[n]
                ext[step, f, X] = plane
            else:
                rhs[step, DEEP + rim(dx, DEEP, slab)[1] + n] = plane

    def unpack_x(step, part, dx):
        m = (dx + 1) // 2
        for n in range(DEEP):
            if part == 0:
                f, X = field_planes(dx, True)[n]
            else:
                X = DEEP + rim(dx, DEEP, slab)[1] + n
            for c in range(rows // 8):
                piece = slice(ROW + 8 * c, ROW + 8 * c + 8)
                value = x_recv[step, part, m, n, c]
                if part == 0:
                    ext[step, f, X, piece] = value
                else:
                    rhs[step, X, piece] = value

    def unpack_corner(step, part, dx, dy):
        m = (dx + 1) + (dy + 1) // 2
        w = 1 if part == 0 else DEEP - 1
        x, y = rim(dx, w, slab)[1], ROW + rim(dy, w, rows)[1]
        if part == 0:
            for f in range(2):
                ext[step, f, 2 + x, y:y + 1] = c_recv[step, part, m, f:f + 1]
        else:
            for n in range(w):
                rhs[step, DEEP + x + n, y:y + w] = c_recv[step, part, m, w * n:w * n + w]

    def arrive_all(step, part):
        flat = flattened(step, part)
        for dy in (-1, 1):
            messages(step, part, 0, dy).wait_recv()
            for n, base in enumerate(lines(part, dy, True)):
                flat[pl.ds(base, slab, stride=TALL), :] = y_recv[step, part, (dy + 1) // 2, n]
        for dx in (-1, 1):
            @pl.when(has[-dx])
            def _():
                messages(step, part, dx, 0).wait_recv()
                unpack_x(step, part, dx)
                for dy in (-1, 1):
                    messages(step, part, dx, dy).wait_recv()
                    unpack_corner(step, part, dx, dy)
        for dx in (-1, 1):
            @pl.when(ends[-dx])
            def _():
                for k in range(ngy):
                    shear_arrival(step, part, -dx, k).wait_recv()
                sheared(step, part, dx)

    def sent_all(step, part):
        for dy in (-1, 1):
            messages(step, part, 0, dy).wait_send()
        for dx in (-1, 1):
            @pl.when(has[dx])
            def _():
                for dy in (0, -1, 1):
                    messages(step, part, dx, dy).wait_send()

            @pl.when(ends[dx])
            def _():
                for k in range(ngy):
                    shear_message(step, part, dx, k).wait_send()

    half = -0.5 * time_step
    keep = 1.0 - 6.0 * time_step * viscosity
    spread = time_step * viscosity

    def move(c, parts, hu, hv, hw):
        total, ddx, ddy, ddz = parts
        return (keep * c + spread * total) + (hu * ddx + hv * ddy + hw * ddz)

    def mean_flow(x):
        return rate * (x.astype(jnp.float32) + (0.5 - total_x / 2.0))

    lo, hi = ROW, ROW + rows

    def provisional(step):
        e = ext.at[step]

        def around(f, X):
            c = e[f, X, lo:hi]
            return c, stencil(c, e[f, X - 1, lo:hi], e[f, X + 1, lo:hi],
                              e[f, X, lo - 1:hi - 1], e[f, X, lo + 1:hi + 1])

        def speeds(X):
            flow = mean_flow(lax.rem(gx * slab + (X - 2) + total_x, total_x))
            u, v, w = e[0, X, lo:hi], e[1, X, lo:hi], e[2, X, lo:hi]
            return u, half * u, half * (v + flow), half * w

        def plane(i, _):
            X = i + 2
            u, hu, hv, hw = speeds(X)
            for f in range(4):
                c, parts = around(f, X)
                value = move(c, parts, hu, hv, hw)
                if f == 1:
                    value = value - (time_step * rate) * u
                if f == 3:
                    value = value - time_step * u
                prov[f, i + 1, lo:hi] = value
            return 0

        lax.fori_loop(0, slab, plane, 0)
        for X in (1, slab + 2):
            u, hu, hv, hw = speeds(X)
            c, parts = around(0, X)
            prov[0, X - 1, lo:hi] = move(c, parts, hu, hv, hw)
        flat = e.reshape(4 * (slab + 4) * TALL, 128)
        into = prov.reshape(4 * (slab + 2) * TALL, 128)
        place = gx * slab + lax.broadcasted_iota(jnp.int32, (slab, 128), 0)
        flow = mean_flow(place)
        for y in (-1, rows):
            def line(f, x, yy):
                return flat[pl.ds((f * (slab + 4) + 2 + x) * TALL + ROW + yy, slab, stride=TALL), :]

            u, c, w = line(0, 0, y), line(1, 0, y), line(2, 0, y)
            parts = stencil(c, line(1, -1, y), line(1, 1, y), line(1, 0, y - 1), line(1, 0, y + 1))
            value = move(c, parts, half * u, half * (c + flow), half * w) - (time_step * rate) * u
            into[pl.ds((slab + 2 + 1) * TALL + ROW + y, slab, stride=TALL), :] = value

    def divergence(step):
        scale = 0.5 / (6.0 * time_step)

        def plane(i, _):
            dx = prov[0, i + 2, lo:hi] - prov[0, i, lo:hi]
            dy = prov[1, i + 1, lo + 1:hi + 1] - prov[1, i + 1, lo - 1:hi - 1]
            w = prov[2, i + 1, lo:hi]
            rhs[step, DEEP + i, lo:hi] = scale * (dx + dy + (across(w, -1) - across(w, 1)))
            return 0

        lax.fori_loop(0, slab, plane, 0)

    def relax(step):
        r = rhs.at[step]
        top, bottom = ROW - RELAX, ROW + rows + RELAX

        def first(X, _):
            c = r[X, top:bottom]
            total = stencil(c, r[X - 1, top:bottom], r[X + 1, top:bottom],
                            r[X, top - 1:bottom - 1], r[X, top + 1:bottom + 1])[0]
            press[0, X, top:bottom] = -(total * (1.0 / 6.0) + c)
            return 0

        lax.fori_loop(1, slab + 2 * DEEP - 1, first, 0)
        for k in range(1, RELAX):
            old, new = press.at[k - 1], press.at[k]

            def sweep(X, _):
                c = old[X, top:bottom]
                total = stencil(c, old[X - 1, top:bottom], old[X + 1, top:bottom],
                                old[X, top - 1:bottom - 1], old[X, top + 1:bottom + 1])[0]
                new[X, top:bottom] = total * (1.0 / 6.0) - r[X, top:bottom]
                return 0

            lax.fori_loop(1 + k, slab + 2 * DEEP - 1 - k, sweep, 0)

    def project(step, store):
        p = press.at[RELAX - 1]

        def plane(i, _):
            X = DEEP + i
            c = p[X, lo:hi]
            store(0, i, prov[0, i + 1, lo:hi] + half * (p[X + 1, lo:hi] - p[X - 1, lo:hi]))
            store(1, i, prov[1, i + 1, lo:hi] + half * (p[X, lo + 1:hi + 1] - p[X, lo - 1:hi - 1]))
            store(2, i, prov[2, i + 1, lo:hi] + half * (across(c, -1) - across(c, 1)))
            store(3, i, prov[3, i + 1, lo:hi])
            return 0

        lax.fori_loop(0, slab, plane, 0)

    fetch.wait()
    for step in range(steps):
        pack(step, 0)
        if step == 0:
            inner = jnp.logical_and(gx > 0, gx < ngx - 1)

            @pl.when(inner)
            def _():
                pl.semaphore_wait(barrier, 8)

            @pl.when(jnp.logical_not(inner))
            def _():
                pl.semaphore_wait(barrier, 5 + ngy)

        start_all(step, 0)
        arrive_all(step, 0)
        provisional(step)
        divergence(step)
        pack(step, 1)
        start_all(step, 1)
        arrive_all(step, 1)
        relax(step)
        if step < steps - 1:
            def store(f, i, value, step=step):
                ext[step + 1, f, i + 2, lo:hi] = value
        else:
            def store(f, i, value):
                final[f, i] = value
        project(step, store)

    give = pltpu.make_async_copy(final, out, local_sem.at[1])
    give.start()
    for step in range(steps):
        for part in range(2):
            sent_all(step, part)
    give.wait()


def local(ngx, ngy, state, offsets):
    steps = offsets.shape[0]
    fields, slab, rows, depth = state.shape
    f32 = jnp.float32
    return pl.pallas_call(
        functools.partial(kernel, ngx, ngy, steps),
        out_shape=jax.ShapeDtypeStruct(state.shape, f32),
        in_specs=[pl.BlockSpec(memory_space=pltpu.SMEM), pl.BlockSpec(memory_space=pl.ANY)],
        out_specs=pl.BlockSpec(memory_space=pl.ANY),
        scratch_shapes=[
            pltpu.VMEM((steps, fields, slab + 4, TALL, depth), f32),
            pltpu.VMEM((fields, slab + 2, TALL, depth), f32),
            pltpu.VMEM((steps, slab + 2 * DEEP, TALL, depth), f32),
            pltpu.VMEM((RELAX, slab + 2 * DEEP, TALL, depth), f32),
            pltpu.VMEM(state.shape, f32),
            pltpu.VMEM((steps, 2, 2, DEEP, rows // 8, 8, depth), f32),
            pltpu.VMEM((steps, 2, 2, DEEP, rows // 8, 8, depth), f32),
            pltpu.VMEM((steps, 2, 2, DEEP, slab, depth), f32),
            pltpu.VMEM((steps, 2, 2, DEEP, slab, depth), f32),
            pltpu.VMEM((steps, 2, 4, 16, depth), f32),
            pltpu.VMEM((steps, 2, 4, 16, depth), f32),
            pltpu.SemaphoreType.DMA((steps, 2, 8)),
            pltpu.SemaphoreType.DMA((steps, 2, 8)),
            pltpu.SemaphoreType.DMA((steps, 2, ngy)),
            pltpu.SemaphoreType.DMA((steps, 2, ngy)),
            pltpu.SemaphoreType.DMA((2,)),
        ] + [pltpu.VMEM((DEEP, ngy * rows // 8, 8, depth), f32)] * (2 * steps),
        compiler_params=pltpu.CompilerParams(
            collective_id=0, has_side_effects=True, vmem_limit_bytes=32 * 1024 * 1024
        ),
    )(offsets, state)


def solution(mesh):
    in_specs = (P(None, "gx", "gy", None), P())
    out_specs = P(None, "gx", "gy", None)
    body = functools.partial(local, mesh.shape["gx"], mesh.shape["gy"])
    return jax.shard_map(body, mesh=mesh, in_specs=in_specs, out_specs=out_specs, check_vma=False)
```

time: 598 us -> 62.6 us (0.10)
  blocking collectives: 398 us -> 0 us
  starting transfers between devices: 135 us -> 0 us
  Pallas kernels: 0 us -> 59.9 us
  waiting for transfers between devices: 47.4 us -> 0 us
    all_gather x14 -> x0, blocking collectives: 398 us -> none  [move_rows(): whole = lax.all_gather(planes, 'gy', axis=2, tiled=True)]
    ppermute x56 -> x0, starting transfers between devices: 135 us -> none  [the longest x28 76.9 us: from_behind(): return lax.ppermute(value, axis, pairs)]
    pallas_call x0 -> x1, Pallas kernels: none -> 59.9 us  [local(): pl.pallas_call(functools.partial(kernel, ngx, ngy, steps), out_shape=jax....]
    ppermute x56 -> x0, waiting for transfers between devices: 47.4 us -> none  [the longest x14 26.6 us: extended(): before = lax.ppermute(last, axis, up)]
  transfers between devices with their start and end apart: 56 -> 0, of which waited for: 30 -> 0; matrix products, arithmetic and copies ran while one was open for 1% -> 0% of each run, Pallas kernels for 0% -> 0%
where the time goes in v1:
time: 62.6 us; the launch traced here: 62.4 us
  Pallas kernels  59.9 us (96%)
  local copies, waits for them, and re-layouts  2.49 us (4%)
    pallas_call x1, Pallas kernels, local(): pl.pallas_call(functools.partial(kernel, ngx, ngy, steps), out_shape=jax....  59.9 us
    unnamed x5, local copies, waits for them, and re-layouts  2.49 us

profile of v1, /device:TPU:0, one launch (start us, length us, event | category | flops | bytes accessed | tf_op | source)
XLA Modules:
  0.0 62.4 jit_solution(2419222529623562304)
XLA Ops:
  0.0 0.0 copy-start
  0.0 1.0 %copy-done = f32[4,16,16,128]{3,2,1,0:T(8,128)S(1)} copy-done((f32[4,16,16,128]{3,2,1,0:T(8,128)S(1)}, f32[4,16,16,128]{3,2,1,0:T(8,128)}, u32[]{:S(2)}) %copy-start) | copy-done | bytes 524312
  1.0 0.0 copy-start.1
  1.0 0.7 %copy-done.1 = s32[2]{0:T(128)S(1)} copy-done((s32[2]{0:T(128)S(1)}, s32[2]{0:T(128)}, u32[]{:S(2)}) %copy-start.1) | copy-done | bytes 32
  1.7 59.9 %shard_map.28 = f32[4,16,16,128]{3,2,1,0:T(8,128)S(1)} custom-call(s32[2]{0:T(128)S(1)} %copy-done.1, f32[4,16,16,128]{3,2,1,0:T(8,128)S(1)} %copy-done), custom_call_target="tpu_custom_call" | custom-call | tf_op jit(solution)/shard_map/pallas_call | solution.py:389
  61.6 0.8 %copy.4 = f32[4,16,16,128]{3,2,1,0:T(8,128)} copy(f32[4,16,16,128]{3,2,1,0:T(8,128)S(1)} %shard_map.28) | data formatting | bytes 1048576
Async XLA Ops:
  0.0 1.0 %copy-start = (f32[4,16,16,128]{3,2,1,0:T(8,128)S(1)}, f32[4,16,16,128]{3,2,1,0:T(8,128)}, u32[]{:S(2)}) copy-start(f32[4,16,16,128]{3,2,1,0:T(8,128)} %state.1) | copy-start | bytes 1572868
  1.0 0.7 %copy-start.1 = (s32[2]{0:T(128)S(1)}, s32[2]{0:T(128)}, u32[]{:S(2)}) copy-start(s32[2]{0:T(128)} %offsets.1) | copy-start | bytes 28

commit v2 on v1

--- a/solution.py
+++ b/solution.py
@@ -26,6 +26,11 @@
     zp, zm = across(c, -1), across(c, 1)
     total = (xp + xm) + (yp + ym) + (zp + zm)
     return total, xp - xm, yp - ym, zp - zm
+
+
+def loop(first, last, body):
+    for n in range(first, last):
+        body(n, 0)
 
 
 def kernel(ngx, ngy, steps, offsets, state, out, ext, prov, rhs, press, final,
@@ -276,7 +281,7 @@
                 prov[f, i + 1, lo:hi] = value
             return 0
 
-        lax.fori_loop(0, slab, plane, 0)
+        loop(0, slab, plane)
         for X in (1, slab + 2):
             u, hu, hv, hw = speeds(X)
             c, parts = around(0, X)
@@ -304,7 +309,7 @@
             rhs[step, DEEP + i, lo:hi] = scale * (dx + dy + (across(w, -1) - across(w, 1)))
             return 0
 
-        lax.fori_loop(0, slab, plane, 0)
+        loop(0, slab, plane)
 
     def relax(step):
         r = rhs.at[step]
@@ -317,7 +322,7 @@
             press[0, X, top:bottom] = -(total * (1.0 / 6.0) + c)
             return 0
 
-        lax.fori_loop(1, slab + 2 * DEEP - 1, first, 0)
+        loop(1, slab + 2 * DEEP - 1, first)
         for k in range(1, RELAX):
             old, new = press.at[k - 1], press.at[k]
 
@@ -328,7 +333,7 @@
                 new[X, top:bottom] = total * (1.0 / 6.0) - r[X, top:bottom]
                 return 0
 
-            lax.fori_loop(1 + k, slab + 2 * DEEP - 1 - k, sweep, 0)
+            loop(1 + k, slab + 2 * DEEP - 1 - k, sweep)
 
     def project(step, store):
         p = press.at[RELAX - 1]
@@ -342,7 +347,7 @@
             store(3, i, prov[3, i + 1, lo:hi])
             return 0
 
-        lax.fori_loop(0, slab, plane, 0)
+        loop(0, slab, plane)
 
     fetch.wait()
     for step in range(steps):

time: 62.6 us -> 44.2 us (0.71)
  Pallas kernels: 59.9 us -> 41.6 us
    pallas_call x1, Pallas kernels: 59.9 us -> 41.6 us  [local(): pl.pallas_call(functools.partial(kernel, ngx, ngy, steps), out_shape=jax....]
where the time goes in v2:
time: 44.2 us; the launch traced here: 44.1 us
  Pallas kernels  41.6 us (94%)
  local copies, waits for them, and re-layouts  2.49 us (6%)
    pallas_call x1, Pallas kernels, local(): pl.pallas_call(functools.partial(kernel, ngx, ngy, steps), out_shape=jax....  41.6 us
    unnamed x5, local copies, waits for them, and re-layouts  2.49 us

profile of v2, /device:TPU:0, one launch (start us, length us, event | category | flops | bytes accessed | tf_op | source)
XLA Modules:
  0.0 44.1 jit_solution(13361277648707611629)
XLA Ops:
  0.0 0.0 copy-start
  0.0 1.0 %copy-done = f32[4,16,16,128]{3,2,1,0:T(8,128)S(1)} copy-done((f32[4,16,16,128]{3,2,1,0:T(8,128)S(1)}, f32[4,16,16,128]{3,2,1,0:T(8,128)}, u32[]{:S(2)}) %copy-start) | copy-done | bytes 524312
  1.0 0.0 copy-start.1
  1.0 0.7 %copy-done.1 = s32[2]{0:T(128)S(1)} copy-done((s32[2]{0:T(128)S(1)}, s32[2]{0:T(128)}, u32[]{:S(2)}) %copy-start.1) | copy-done | bytes 32
  1.7 41.6 %shard_map.28 = f32[4,16,16,128]{3,2,1,0:T(8,128)S(1)} custom-call(s32[2]{0:T(128)S(1)} %copy-done.1, f32[4,16,16,128]{3,2,1,0:T(8,128)S(1)} %copy-done), custom_call_target="tpu_custom_call" | custom-call | tf_op jit(solution)/shard_map/pallas_call | solution.py:394
  43.3 0.8 %copy.4 = f32[4,16,16,128]{3,2,1,0:T(8,128)} copy(f32[4,16,16,128]{3,2,1,0:T(8,128)S(1)} %shard_map.28) | data formatting | bytes 1048576
Async XLA Ops:
  0.0 1.0 %copy-start = (f32[4,16,16,128]{3,2,1,0:T(8,128)S(1)}, f32[4,16,16,128]{3,2,1,0:T(8,128)}, u32[]{:S(2)}) copy-start(f32[4,16,16,128]{3,2,1,0:T(8,128)} %state.1) | copy-start | bytes 1572868
  1.0 0.7 %copy-start.1 = (s32[2]{0:T(128)S(1)}, s32[2]{0:T(128)}, u32[]{:S(2)}) copy-start(s32[2]{0:T(128)} %offsets.1) | copy-start | bytes 28

commit v3 on v1

v3 whole, which is shorter than its diff:
```python
import functools

import jax
import jax.numpy as jnp
from jax import lax
from jax.experimental import pallas as pl
from jax.experimental.pallas import tpu as pltpu
from jax.sharding import PartitionSpec as P

RELAX = 4
DEEP = RELAX + 1

time_step = 0.2
viscosity = 0.1

MESH = pl.DeviceIdType.MESH
ROW = 8
TALL = 32


def across(x, shift):
    return pltpu.roll(x, shift % x.shape[-1], x.ndim - 1)


def stencil(c, xm, xp, ym, yp):
    zp, zm = across(c, -1), across(c, 1)
    total = (xp + xm) + (yp + ym) + (zp + zm)
    return total, xp - xm, yp - ym, zp - zm


def kernel(ngx, ngy, steps, offsets_in, state, out, ext, prov, rhs, press,
           x_send, x_recv, y_send, y_recv, c_send, c_recv, send_sem, recv_sem, shear_out, shear_in, local_sem, offsets, *shear_recv):
    slab, rows = state.shape[1], state.shape[2]
    gx, gy = lax.axis_index("gx"), lax.axis_index("gy")
    below, above = lax.rem(gx + ngx - 1, ngx), lax.rem(gx + 1, ngx)
    left, right = lax.rem(gy + ngy - 1, ngy), lax.rem(gy + 1, ngy)
    at_x = {-1: below, 0: gx, 1: above}
    at_y = {-1: left, 0: gy, 1: right}
    has = {-1: gx > 0, 1: gx < ngx - 1}
    ends = {-1: gx == 0, 1: gx == ngx - 1}
    far = {-1: ngx - 1, 1: 0}
    total_x = slab * ngx
    rate = 2.0 / total_x
    own = pl.ds(ROW, rows)

    fetch = pltpu.make_async_copy(state, ext.at[0, :, pl.ds(2, slab), own, :], local_sem.at[0])
    fetch.start()
    fetch_offsets = pltpu.make_async_copy(offsets_in, offsets, local_sem.at[2])
    fetch_offsets.start()

    barrier = pltpu.get_barrier_semaphore()

    def greet(x, y):
        pl.semaphore_signal(barrier, inc=1, device_id=(x, y), device_id_type=MESH)

    for dy in (-1, 1):
        greet(gx, at_y[dy])
    for dx in (-1, 1):
        @pl.when(has[dx])
        def _():
            for dy in (-1, 0, 1):
                greet(at_x[dx], at_y[dy])

        @pl.when(ends[dx])
        def _():
            for k in range(ngy):
                greet(far[dx], k)

    def remote(src, dst, send, recv, x, y):
        return pltpu.make_async_remote_copy(
            src_ref=src, dst_ref=dst, send_sem=send, recv_sem=recv,
            device_id=(x, y), device_id_type=MESH)

    def rim(side, width, size):
        return (0, size) if side < 0 else (size - width, -width)

    def messages(step, part, dx, dy):
        dev = at_x[dx], at_y[dy]
        if dx == 0:
            n = m = (dy + 1) // 2
            src, dst = y_send.at[step, part, m], y_recv.at[step, part, m]
        elif dy == 0:
            m = (dx + 1) // 2
            n = 2 + m
            src, dst = x_send.at[step, part, m], x_recv.at[step, part, m]
        else:
            m = (dx + 1) + (dy + 1) // 2
            n = 4 + m
            size = pl.ds(0, 8 if part == 0 else 16)
            src, dst = c_send.at[step, part, m, size, :], c_recv.at[step, part, m, size, :]
        return remote(src, dst, send_sem.at[step, part, n], recv_sem.at[step, part, n], *dev)

    def shear_part(kind, dx):
        if kind == 0:
            return 0, DEEP
        deep = DEEP - 2
        if kind == 1:
            return (2 if dx < 0 else 0), deep
        return (0 if dx < 0 else deep), 2

    def shear_slot(step, kind, k):
        return shear_recv[3 * step + kind].at[:, pl.ds(k * (rows // 8), rows // 8), :, :]

    def shear_message(step, kind, dx, k):
        first, count = shear_part(kind, dx)
        src = x_send.at[step, min(kind, 1), (dx + 1) // 2, pl.ds(first, count)]
        return remote(src, shear_slot(step, kind, gy),
                      shear_out.at[step, kind, k], shear_in.at[step, kind, gy], far[dx], k)

    def shear_arrival(step, kind, dx, k):
        slot = shear_slot(step, kind, k)
        return remote(slot, slot, shear_out.at[step, kind, k], shear_in.at[step, kind, k], far[dx], k)

    def field_planes(dx, ghost):
        s2, d2 = rim(dx, 2, slab)
        s1, d1 = rim(dx, 1, slab)
        p2, p1 = (d2, d1) if ghost else (s2, s1)
        return [(0, 2 + p2), (0, 3 + p2), (1, 2 + p1), (2, 2 + p1), (3, 2 + p1)]

    def lines(part, dy, ghost):
        if part == 0:
            s2, d2 = rim(dy, 2, rows)
            s1, d1 = rim(dy, 1, rows)
            p2, p1 = (d2, d1) if ghost else (s2, s1)
            return [(f * (slab + 4) + 2) * TALL + ROW + y
                    for f, y in ((1, p2), (1, p2 + 1), (0, p1), (2, p1), (3, p1))]
        s, d = rim(dy, DEEP, rows)
        return [DEEP * TALL + ROW + (d if ghost else s) + k for k in range(DEEP)]

    def flattened(step, part):
        if part == 0:
            return ext.at[step].reshape(4 * (slab + 4) * TALL, 128)
        return rhs.at[step].reshape((slab + 2 * DEEP) * TALL, 128)

    def pack_x(step, part, dx, first=0, count=DEEP):
        m = (dx + 1) // 2
        for n in range(first, first + count):
            if part == 0:
                f, X = field_planes(dx, False)[n]
            else:
                X = DEEP + rim(dx, DEEP, slab)[0] + n
            for c in range(rows // 8):
                piece = slice(ROW + 8 * c, ROW + 8 * c + 8)
                x_send[step, part, m, n, c] = ext[step, f, X, piece] if part == 0 else rhs[step, X, piece]

    def pack_y(step, part, dy):
        flat = flattened(step, part)
        for n, base in enumerate(lines(part, dy, False)):
            y_send[step, part, (dy + 1) // 2, n] = flat[pl.ds(base, slab, stride=TALL), :]

    def pack_corner(step, part, dx, dy):
        w = 1 if part == 0 else DEEP - 1
        m = (dx + 1) + (dy + 1) // 2
        x, y = rim(dx, w, slab)[0], ROW + rim(dy, w, rows)[0]
        if part == 0:
            for f in range(2):
                c_send[step, part, m, f:f + 1] = ext[step, f, 2 + x, y:y + 1]
        else:
            for n in range(w):
                c_send[step, part, m, w * n:w * n + w] = rhs[step, DEEP + x + n, y:y + w]

    def start_shear(step, kind):
        for dx in (-1, 1):
            @pl.when(ends[dx])
            def _():
                if kind > 0:
                    pack_x(step, 1, dx, *shear_part(kind, dx))
                else:
                    pack_x(step, 0, dx)
                for k in range(ngy):
                    shear_message(step, kind, dx, k).start()

    def start_x(step, part):
        for dx in (-1, 1):
            @pl.when(has[dx])
            def _():
                pack_x(step, part, dx)
                messages(step, part, dx, 0).start()
                for dy in (-1, 1):
                    pack_corner(step, part, dx, dy)
                    messages(step, part, dx, dy).start()

    def start_y(step, part):
        for dy in (-1, 1):
            pack_y(step, part, dy)
            messages(step, part, 0, dy).start()

    def sheared(step, kind, dx):
        span = rows * ngy
        shift = span - offsets[step] if dx > 0 else offsets[step]
        start = lax.rem(gy * rows + shift + (span - ROW), span)
        block, within = lax.div(start, 8), lax.rem(start, 8)
        blocks = [lax.rem(block + c, span // 8) for c in range(TALL // 8 + 1)]
        first, count = shear_part(kind, dx)
        for n in range(first, first + count):
            tall = jnp.concatenate([shear_recv[3 * step + kind][n - first, at] for at in blocks], axis=0)
            plane = pltpu.roll(tall, TALL + 8 - within, 0)[:TALL]
            if kind == 0:
                f, X = field_planes(dx, True)[n]
                ext[step, f, X] = plane
            else:
                rhs[step, DEEP + rim(dx, DEEP, slab)[1] + n] = plane

    def unpack_x(step, part, dx):
        m = (dx + 1) // 2
        for n in range(DEEP):
            if part == 0:
                f, X = field_planes(dx, True)[n]
            else:
                X = DEEP + rim(dx, DEEP, slab)[1] + n
            for c in range(rows // 8):
                piece = slice(ROW + 8 * c, ROW + 8 * c + 8)
                value = x_recv[step, part, m, n, c]
                if part == 0:
                    ext[step, f, X, piece] = value
                else:
                    rhs[step, X, piece] = value

    def unpack_corner(step, part, dx, dy):
        m = (dx + 1) + (dy + 1) // 2
        w = 1 if part == 0 else DEEP - 1
        x, y = rim(dx, w, slab)[1], ROW + rim(dy, w, rows)[1]
        if part == 0:
            for f in range(2):
                ext[step, f, 2 + x, y:y + 1] = c_recv[step, part, m, f:f + 1]
        else:
            for n in range(w):
                rhs[step, DEEP + x + n, y:y + w] = c_recv[step, part, m, w * n:w * n + w]

    def arrive_y(step, part):
        flat = flattened(step, part)
        for dy in (-1, 1):
            messages(step, part, 0, dy).wait_recv()
            for n, base in enumerate(lines(part, dy, True)):
                flat[pl.ds(base, slab, stride=TALL), :] = y_recv[step, part, (dy + 1) // 2, n]

    def arrive_x(step, part):
        for dx in (-1, 1):
            @pl.when(has[-dx])
            def _():
                messages(step, part, dx, 0).wait_recv()
                unpack_x(step, part, dx)
                for dy in (-1, 1):
                    messages(step, part, dx, dy).wait_recv()
                    unpack_corner(step, part, dx, dy)
        for dx in (-1, 1):
            @pl.when(ends[-dx])
            def _():
                for kind in ((0,) if part == 0 else (1, 2)):
                    for k in range(ngy):
                        shear_arrival(step, kind, -dx, k).wait_recv()
                    sheared(step, kind, dx)

    def sent_all(step):
        for part in range(2):
            for dy in (-1, 1):
                messages(step, part, 0, dy).wait_send()
            for dx in (-1, 1):
                @pl.when(has[dx])
                def _():
                    for dy in (0, -1, 1):
                        messages(step, part, dx, dy).wait_send()
        for dx in (-1, 1):
            @pl.when(ends[dx])
            def _():
                for kind in range(3):
                    for k in range(ngy):
                        shear_message(step, kind, dx, k).wait_send()

    half = -0.5 * time_step
    keep = 1.0 - 6.0 * time_step * viscosity
    spread = time_step * viscosity

    def move(c, parts, hu, hv, hw):
        total, ddx, ddy, ddz = parts
        return (keep * c + spread * total) + (hu * ddx + hv * ddy + hw * ddz)

    def mean_flow(x):
        return rate * (x.astype(jnp.float32) + (0.5 - total_x / 2.0))

    lo, hi = ROW, ROW + rows

    def speeds(step, X):
        e = ext.at[step]
        flow = mean_flow(lax.rem(gx * slab + (X - 2) + total_x, total_x))
        u, v, w = e[0, X, lo:hi], e[1, X, lo:hi], e[2, X, lo:hi]
        return u, half * u, half * (v + flow), half * w

    def around(step, f, X):
        e = ext.at[step]
        c = e[f, X, lo:hi]
        return c, stencil(c, e[f, X - 1, lo:hi], e[f, X + 1, lo:hi],
                          e[f, X, lo - 1:hi - 1], e[f, X, lo + 1:hi + 1])

    def provisional(step, planes):
        for i in planes:
            X = i + 2
            u, hu, hv, hw = speeds(step, X)
            for f in range(4):
                c, parts = around(step, f, X)
                value = move(c, parts, hu, hv, hw)
                if f == 1:
                    value = value - (time_step * rate) * u
                if f == 3:
                    value = value - time_step * u
                prov[f, i + 1, lo:hi] = value

    def provisional_x_ghosts(step):
        for X in (1, slab + 2):
            u, hu, hv, hw = speeds(step, X)
            c, parts = around(step, 0, X)
            prov[0, X - 1, lo:hi] = move(c, parts, hu, hv, hw)

    def provisional_y_ghosts(step):
        flat = flattened(step, 0)
        into = prov.reshape(4 * (slab + 2) * TALL, 128)
        place = gx * slab + lax.broadcasted_iota(jnp.int32, (slab, 128), 0)
        flow = mean_flow(place)
        for y in (-1, rows):
            def line(f, x, yy):
                return flat[pl.ds((f * (slab + 4) + 2 + x) * TALL + ROW + yy, slab, stride=TALL), :]

            u, c, w = line(0, 0, y), line(1, 0, y), line(2, 0, y)
            parts = stencil(c, line(1, -1, y), line(1, 1, y), line(1, 0, y - 1), line(1, 0, y + 1))
            value = move(c, parts, half * u, half * (c + flow), half * w) - (time_step * rate) * u
            into[pl.ds((slab + 2 + 1) * TALL + ROW + y, slab, stride=TALL), :] = value

    def divergence(step, planes):
        scale = 0.5 / (6.0 * time_step)
        for i in planes:
            dx = prov[0, i + 2, lo:hi] - prov[0, i, lo:hi]
            dy = prov[1, i + 1, lo + 1:hi + 1] - prov[1, i + 1, lo - 1:hi - 1]
            w = prov[2, i + 1, lo:hi]
            rhs[step, DEEP + i, lo:hi] = scale * (dx + dy + (across(w, -1) - across(w, 1)))

    def relax(step, k, planes):
        r = rhs.at[step]
        top, bottom = ROW - RELAX, ROW + rows + RELAX
        old, new = (press.at[k - 1] if k else r), press.at[k]
        for x in planes:
            X = DEEP + x
            c = old[X, top:bottom]
            total = stencil(c, old[X - 1, top:bottom], old[X + 1, top:bottom],
                            old[X, top - 1:bottom - 1], old[X, top + 1:bottom + 1])[0]
            if k == 0:
                new[X, top:bottom] = -(total * (1.0 / 6.0) + c)
            else:
                new[X, top:bottom] = total * (1.0 / 6.0) - r[X, top:bottom]

    def project(step, planes):
        p = press.at[RELAX - 1]

        def store(f, i, value):
            if step < steps - 1:
                ext[step + 1, f, i + 2, lo:hi] = value
            else:
                out[f, i] = value

        for i in planes:
            X = DEEP + i
            c = p[X, lo:hi]
            store(0, i, prov[0, i + 1, lo:hi] + half * (p[X + 1, lo:hi] - p[X - 1, lo:hi]))
            store(1, i, prov[1, i + 1, lo:hi] + half * (p[X, lo + 1:hi + 1] - p[X, lo - 1:hi - 1]))
            store(2, i, prov[2, i + 1, lo:hi] + half * (across(c, -1) - across(c, 1)))
            store(3, i, prov[3, i + 1, lo:hi])

    fetch.wait()
    inner = jnp.logical_and(gx > 0, gx < ngx - 1)

    @pl.when(inner)
    def _():
        pl.semaphore_wait(barrier, 8)

    @pl.when(jnp.logical_not(inner))
    def _():
        pl.semaphore_wait(barrier, 5 + ngy)

    for step in range(steps):
        if step == 0:
            start_shear(step, 0)
            start_x(step, 0)
            start_y(step, 0)
            fetch_offsets.wait()
        arrive_y(step, 0)
        provisional(step, range(1, slab - 1))
        provisional_y_ghosts(step)
        divergence(step, range(2, slab - 2))
        start_shear(step, 1)
        arrive_x(step, 0)
        provisional(step, (0, slab - 1))
        provisional_x_ghosts(step)
        provisional_y_ghosts(step)
        divergence(step, (0, 1, slab - 2, slab - 1))
        start_shear(step, 2)
        start_x(step, 1)
        start_y(step, 1)
        arrive_y(step, 1)
        for k in range(RELAX):
            relax(step, k, range(k + 1, slab - k - 1))
        early = range(RELAX + 1, slab - RELAX - 1)
        project(step, early)
        arrive_x(step, 1)
        for k in range(RELAX):
            relax(step, k, range(k - RELAX, k + 1))
            relax(step, k, range(slab - k - 1, slab + RELAX - k))
        ends_first = (0, 1, slab - 2, slab - 1)
        project(step, ends_first)
        if step < steps - 1:
            start_shear(step + 1, 0)
            start_x(step + 1, 0)
        project(step, [i for i in range(slab) if i not in ends_first and i not in early])
        if step < steps - 1:
            start_y(step + 1, 0)

    for step in range(steps):
        sent_all(step)


def local(ngx, ngy, state, offsets):
    steps = offsets.shape[0]
    fields, slab, rows, depth = state.shape
    f32 = jnp.float32
    return pl.pallas_call(
        functools.partial(kernel, ngx, ngy, steps),
        out_shape=jax.ShapeDtypeStruct(state.shape, f32),
        in_specs=[pl.BlockSpec(memory_space=pl.ANY), pl.BlockSpec(memory_space=pl.ANY)],
        out_specs=pl.BlockSpec(memory_space=pltpu.VMEM),
        scratch_shapes=[
            pltpu.VMEM((steps, fields, slab + 4, TALL, depth), f32),
            pltpu.VMEM((fields, slab + 2, TALL, depth), f32),
            pltpu.VMEM((steps, slab + 2 * DEEP, TALL, depth), f32),
            pltpu.VMEM((RELAX, slab + 2 * DEEP, TALL, depth), f32),
            pltpu.VMEM((steps, 2, 2, DEEP, rows // 8, 8, depth), f32),
            pltpu.VMEM((steps, 2, 2, DEEP, rows // 8, 8, depth), f32),
            pltpu.VMEM((steps, 2, 2, DEEP, slab, depth), f32),
            pltpu.VMEM((steps, 2, 2, DEEP, slab, depth), f32),
            pltpu.VMEM((steps, 2, 4, 16, depth), f32),
            pltpu.VMEM((steps, 2, 4, 16, depth), f32),
            pltpu.SemaphoreType.DMA((steps, 2, 8)),
            pltpu.SemaphoreType.DMA((steps, 2, 8)),
            pltpu.SemaphoreType.DMA((steps, 3, ngy)),
            pltpu.SemaphoreType.DMA((steps, 3, ngy)),
            pltpu.SemaphoreType.DMA((3,)),
            pltpu.SMEM((steps,), jnp.int32),
        ] + [pltpu.VMEM((count, ngy * rows // 8, 8, depth), f32) for count in (DEEP, DEEP - 2, 2)] * steps,
        compiler_params=pltpu.CompilerParams(
            collective_id=0, has_side_effects=True, vmem_limit_bytes=32 * 1024 * 1024
        ),
    )(offsets, state)


def solution(mesh):
    in_specs = (P(None, "gx", "gy", None), P())
    out_specs = P(None, "gx", "gy", None)
    body = functools.partial(local, mesh.shape["gx"], mesh.shape["gy"])
    return jax.shard_map(body, mesh=mesh, in_specs=in_specs, out_specs=out_specs, check_vma=False)
```

time: 62.6 us -> 40.5 us (0.65)
  Pallas kernels: 59.9 us -> 37.9 us
    pallas_call x1, Pallas kernels: 59.9 us -> 37.9 us  [local(): pl.pallas_call(functools.partial(kernel, ngx, ngy, steps), out_shape=jax....]
where the time goes in v3:
time: 40.5 us; the launch traced here: 40.4 us
  Pallas kernels  37.9 us (94%)
  local copies, waits for them, and re-layouts  2.49 us (6%)
    pallas_call x1, Pallas kernels, local(): pl.pallas_call(functools.partial(kernel, ngx, ngy, steps), out_shape=jax....  37.9 us
    unnamed x5, local copies, waits for them, and re-layouts  2.49 us

profile of v3, /device:TPU:0, one launch (start us, length us, event | category | flops | bytes accessed | tf_op | source)
XLA Modules:
  0.0 40.4 jit_solution(12589112232306658937)
XLA Ops:
  0.0 0.0 copy-start
  0.0 1.0 %copy-done = f32[4,16,16,128]{3,2,1,0:T(8,128)S(1)} copy-done((f32[4,16,16,128]{3,2,1,0:T(8,128)S(1)}, f32[4,16,16,128]{3,2,1,0:T(8,128)}, u32[]{:S(2)}) %copy-start) | copy-done | bytes 524312
  1.0 0.0 copy-start.1
  1.0 0.7 %copy-done.1 = s32[2]{0:T(128)S(1)} copy-done((s32[2]{0:T(128)S(1)}, s32[2]{0:T(128)}, u32[]{:S(2)}) %copy-start.1) | copy-done | bytes 32
  1.7 37.9 %shard_map.28 = f32[4,16,16,128]{3,2,1,0:T(8,128)S(1)} custom-call(s32[2]{0:T(128)S(1)} %copy-done.1, f32[4,16,16,128]{3,2,1,0:T(8,128)S(1)} %copy-done), custom_call_target="tpu_custom_call" | custom-call | tf_op jit(solution)/shard_map/pallas_call | solution.py:423
  39.6 0.8 %copy.4 = f32[4,16,16,128]{3,2,1,0:T(8,128)} copy(f32[4,16,16,128]{3,2,1,0:T(8,128)S(1)} %shard_map.28) | data formatting | bytes 1048576
Async XLA Ops:
  0.0 1.0 %copy-start = (f32[4,16,16,128]{3,2,1,0:T(8,128)S(1)}, f32[4,16,16,128]{3,2,1,0:T(8,128)}, u32[]{:S(2)}) copy-start(f32[4,16,16,128]{3,2,1,0:T(8,128)} %state.1) | copy-start | bytes 1572868
  1.0 0.7 %copy-start.1 = (s32[2]{0:T(128)S(1)}, s32[2]{0:T(128)}, u32[]{:S(2)}) copy-start(s32[2]{0:T(128)} %offsets_in.1) | copy-start | bytes 28

commit v4 on v3

--- a/solution.py
+++ b/solution.py
@@ -167,8 +167,8 @@
                     pack_x(step, 1, dx, *shear_part(kind, dx))
                 else:
                     pack_x(step, 0, dx)
-                for k in range(ngy):
-                    shear_message(step, kind, dx, k).start()
+                for away in range(ngy):
+                    shear_message(step, kind, dx, lax.rem(gy + away, ngy)).start()
 
     def start_x(step, part):
         for dx in (-1, 1):
@@ -399,6 +399,7 @@
             relax(step, k, range(k + 1, slab - k - 1))
         early = range(RELAX + 1, slab - RELAX - 1)
         project(step, early)
+        sent_all(step)
         arrive_x(step, 1)
         for k in range(RELAX):
             relax(step, k, range(k - RELAX, k + 1))
@@ -411,9 +412,6 @@
         project(step, [i for i in range(slab) if i not in ends_first and i not in early])
         if step < steps - 1:
             start_y(step + 1, 0)
-
-    for step in range(steps):
-        sent_all(step)
 
 
 def local(ngx, ngy, state, offsets):
@@ -444,7 +442,7 @@
             pltpu.SMEM((steps,), jnp.int32),
         ] + [pltpu.VMEM((count, ngy * rows // 8, 8, depth), f32) for count in (DEEP, DEEP - 2, 2)] * steps,
         compiler_params=pltpu.CompilerParams(
-            collective_id=0, has_side_effects=True, vmem_limit_bytes=32 * 1024 * 1024
+            collective_id=0, has_side_effects=True, vmem_limit_bytes=53 * 1024 * 1024 + 256 * 1024
         ),
     )(offsets, state)
 

time: 40.5 us -> 39.1 us (0.965)
  local copies, waits for them, and re-layouts: 2.49 us -> 1.45 us
    unnamed x5 -> x3, local copies, waits for them, and re-layouts: 2.49 us -> 1.45 us
where the time goes in v4:
time: 39.1 us; the launch traced here: 39 us
  Pallas kernels  37.5 us (96%)
  local copies, waits for them, and re-layouts  1.45 us (4%)
    pallas_call x1, Pallas kernels, local(): pl.pallas_call(functools.partial(kernel, ngx, ngy, steps), out_shape=jax....  37.5 us
    unnamed x3, local copies, waits for them, and re-layouts  1.45 us

profile of v4, /device:TPU:0, one launch (start us, length us, event | category | flops | bytes accessed | tf_op | source)
XLA Modules:
  0.0 39.0 jit_solution(15969351603013480536)
XLA Ops:
  0.0 0.0 copy-start
  0.0 0.7 %copy-done = s32[2]{0:T(128)S(1)} copy-done((s32[2]{0:T(128)S(1)}, s32[2]{0:T(128)}, u32[]{:S(2)}) %copy-start) | copy-done | bytes 32
  0.7 37.5 %shard_map.28 = f32[4,16,16,128]{3,2,1,0:T(8,128)S(1)} custom-call(s32[2]{0:T(128)S(1)} %copy-done, f32[4,16,16,128]{3,2,1,0:T(8,128)} %state.1), custom_call_target="tpu_custom_call" | custom-call | tf_op jit(solution)/shard_map/pallas_call | solution.py:421
  38.2 0.8 %copy.4 = f32[4,16,16,128]{3,2,1,0:T(8,128)} copy(f32[4,16,16,128]{3,2,1,0:T(8,128)S(1)} %shard_map.28) | data formatting | bytes 1048576
Async XLA Ops:
  0.0 0.7 %copy-start = (s32[2]{0:T(128)S(1)}, s32[2]{0:T(128)}, u32[]{:S(2)}) copy-start(s32[2]{0:T(128)} %offsets_in.1) | copy-start | bytes 28

commit v5 on v4

--- a/solution.py
+++ b/solution.py
@@ -43,28 +43,28 @@
     rate = 2.0 / total_x
     own = pl.ds(ROW, rows)
 
-    fetch = pltpu.make_async_copy(state, ext.at[0, :, pl.ds(2, slab), own, :], local_sem.at[0])
-    fetch.start()
-    fetch_offsets = pltpu.make_async_copy(offsets_in, offsets, local_sem.at[2])
-    fetch_offsets.start()
-
     barrier = pltpu.get_barrier_semaphore()
 
     def greet(x, y):
         pl.semaphore_signal(barrier, inc=1, device_id=(x, y), device_id_type=MESH)
 
-    for dy in (-1, 1):
-        greet(gx, at_y[dy])
+    for dx in (-1, 1):
+        @pl.when(ends[dx])
+        def _():
+            for k in range(ngy):
+                greet(far[dx], k)
     for dx in (-1, 1):
         @pl.when(has[dx])
         def _():
             for dy in (-1, 0, 1):
                 greet(at_x[dx], at_y[dy])
-
-        @pl.when(ends[dx])
-        def _():
-            for k in range(ngy):
-                greet(far[dx], k)
+    for dy in (-1, 1):
+        greet(gx, at_y[dy])
+
+    fetch = pltpu.make_async_copy(state, ext.at[0, :, pl.ds(2, slab), own, :], local_sem.at[0])
+    fetch.start()
+    fetch_offsets = pltpu.make_async_copy(offsets_in, offsets, local_sem.at[2])
+    fetch_offsets.start()
 
     def remote(src, dst, send, recv, x, y):
         return pltpu.make_async_remote_copy(
@@ -243,6 +243,8 @@
                 for dy in (-1, 1):
                     messages(step, part, dx, dy).wait_recv()
                     unpack_corner(step, part, dx, dy)
+                if part == 1:
+                    finish(step, -dx)
         for dx in (-1, 1):
             @pl.when(ends[-dx])
             def _():
@@ -250,6 +252,8 @@
                     for k in range(ngy):
                         shear_arrival(step, kind, -dx, k).wait_recv()
                     sheared(step, kind, dx)
+                if part == 1:
+                    finish(step, -dx)
 
     def sent_all(step):
         for part in range(2):
@@ -346,6 +350,11 @@
                 new[X, top:bottom] = -(total * (1.0 / 6.0) + c)
             else:
                 new[X, top:bottom] = total * (1.0 / 6.0) - r[X, top:bottom]
+
+    def finish(step, side):
+        for k in range(RELAX):
+            relax(step, k, range(k - RELAX, k + 1) if side < 0 else range(slab - k - 1, slab + RELAX - k))
+        project(step, (0, 1) if side < 0 else (slab - 2, slab - 1))
 
     def project(step, planes):
         p = press.at[RELAX - 1]
@@ -401,15 +410,10 @@
         project(step, early)
         sent_all(step)
         arrive_x(step, 1)
-        for k in range(RELAX):
-            relax(step, k, range(k - RELAX, k + 1))
-            relax(step, k, range(slab - k - 1, slab + RELAX - k))
-        ends_first = (0, 1, slab - 2, slab - 1)
-        project(step, ends_first)
         if step < steps - 1:
             start_shear(step + 1, 0)
             start_x(step + 1, 0)
-        project(step, [i for i in range(slab) if i not in ends_first and i not in early])
+        project(step, [i for i in range(2, slab - 2) if i not in early])
         if step < steps - 1:
             start_y(step + 1, 0)
 
@@ -442,9 +446,9 @@
             pltpu.SMEM((steps,), jnp.int32),
         ] + [pltpu.VMEM((count, ngy * rows // 8, 8, depth), f32) for count in (DEEP, DEEP - 2, 2)] * steps,
         compiler_params=pltpu.CompilerParams(
-            collective_id=0, has_side_effects=True, vmem_limit_bytes=53 * 1024 * 1024 + 256 * 1024
+            collective_id=0, has_side_effects=True, vmem_limit_bytes=32 * 1024 * 1024
         ),
-    )(offsets, state)
+    )(pltpu.with_memory_space_constraint(offsets, pltpu.HBM), pltpu.with_memory_space_constraint(state, pltpu.HBM))
 
 
 def solution(mesh):

time: 39.1 us -> 38.3 us (0.980)
  local copies, waits for them, and re-layouts: 1.45 us -> 0.8 us
    unnamed x3 -> x1, local copies, waits for them, and re-layouts: 1.45 us -> 0.8 us
where the time goes in v5:
time: 38.3 us; the launch traced here: 38.2 us
  Pallas kernels  37.4 us (98%)
  local copies, waits for them, and re-layouts  0.8 us (2%)
    pallas_call x1, Pallas kernels, local(): pl.pallas_call(functools.partial(kernel, ngx, ngy, steps), out_shape=jax....  37.4 us
    unnamed x1, local copies, waits for them, and re-layouts  0.8 us

profile of v5, /device:TPU:0, one launch (start us, length us, event | category | flops | bytes accessed | tf_op | source)
XLA Modules:
  0.0 38.2 jit_solution(2298829041713809572)
XLA Ops:
  0.0 37.4 %shard_map.28 = f32[4,16,16,128]{3,2,1,0:T(8,128)S(1)} custom-call(s32[2]{0:T(128)} %offsets_in.1, f32[4,16,16,128]{3,2,1,0:T(8,128)} %state.1), custom_call_target="tpu_custom_call" | custom-call | tf_op jit(solution)/shard_map/pallas_call | solution.py:425
  37.4 0.8 %copy.4 = f32[4,16,16,128]{3,2,1,0:T(8,128)} copy(f32[4,16,16,128]{3,2,1,0:T(8,128)S(1)} %shard_map.28) | data formatting | bytes 1048576

commit v6 on v5

--- a/solution.py
+++ b/solution.py
@@ -194,7 +194,7 @@
         first, count = shear_part(kind, dx)
         for n in range(first, first + count):
             tall = jnp.concatenate([shear_recv[3 * step + kind][n - first, at] for at in blocks], axis=0)
-            plane = pltpu.roll(tall, TALL + 8 - within, 0)[:TALL]
+            plane = pltpu.roll(tall, lax.rem(TALL + 8 - within, TALL + 8), 0)[:TALL]
             if kind == 0:
                 f, X = field_planes(dx, True)[n]
                 ext[step, f, X] = plane

time: 38.3 us -> 38.3 us (level)
  no operation moved by 1% of the time
where the time goes in v6:
time: 38.3 us; the launch traced here: 38.2 us
  Pallas kernels  37.4 us (98%)
  local copies, waits for them, and re-layouts  0.8 us (2%)
    pallas_call x1, Pallas kernels, local(): pl.pallas_call(functools.partial(kernel, ngx, ngy, steps), out_shape=jax....  37.4 us
    unnamed x1, local copies, waits for them, and re-layouts  0.8 us

profile of v6, /device:TPU:0, one launch (start us, length us, event | category | flops | bytes accessed | tf_op | source)
XLA Modules:
  0.0 38.2 jit_solution(15425873075340697345)
XLA Ops:
  0.0 37.4 %shard_map.28 = f32[4,16,16,128]{3,2,1,0:T(8,128)S(1)} custom-call(s32[2]{0:T(128)} %offsets_in.1, f32[4,16,16,128]{3,2,1,0:T(8,128)} %state.1), custom_call_target="tpu_custom_call" | custom-call | tf_op jit(solution)/shard_map/pallas_call | solution.py:425
  37.4 0.8 %copy.4 = f32[4,16,16,128]{3,2,1,0:T(8,128)} copy(f32[4,16,16,128]{3,2,1,0:T(8,128)S(1)} %shard_map.28) | data formatting | bytes 1048576
